TPU v7x, 256 devices: a whole 4x4x8 slice. The times are simulated.
256 devices in a mesh: dp: 64 (over z, x, core), feat: 4 (over y).
Axes of the slice: x: 4, y: 4, z: 8, core: 2. Of those that a mesh axis runs over, the one named last changes fastest.
Arguments:
- table: int32 [65536, 2048], P('dp', 'feat'), may hold values from 0 to 63
- sample_rows: int32 [32768], P('dp'), may hold values from 0 to 1023
- gradients: bfloat16 [32768, 16], P('dp'), may hold values from -6 to 6
- hessian: bfloat16 [32768], P('dp'), may hold values from 0.0049743652 to 0.049804688
- node_ids: int32 [32768], P('dp'), may hold values from 0 to 1
- split_feature: int32 [2], replicated, may hold values from 0 to 2047
- split_bin: int32 [2], replicated, may hold values from 0 to 63
Outputs:
- best_gain: float32 [2, 2048], P(None, 'feat')
- leaf_values: float32 [4, 16], replicated
Inputs may be any that keep to these rules, and one draw needn't show every extreme that they name: `sample_rows`: each entry names a row of the same device's block of 1024 table rows.
All inputs are finite; a program needn't handle non-finite values.
Results may differ from a plain program's by a relative error of at most 0.0003.
Values sent between devices are 32-bit elements; how exact they have to be, the bound alone decides.
A program may use at most 64 MiB of HBM per device.

v0:
```python
import math

import jax
import jax.numpy as jnp
from jax import lax
from jax.sharding import PartitionSpec as P

BINS = 64
K = 16
NODES = 2


LAMBDA_REG = 1.0
GAIN_WEIGHT = 0.01


def split_gain(left, total):
    grad_left = left[..., :K]
    hess_left = left[..., K]
    grad_total = total[..., :K]
    hess_total = total[..., K]
    grad_right = grad_total - grad_left
    hess_right = hess_total - hess_left
    score = jnp.sum(grad_left * grad_left, axis=-1) / (hess_left + LAMBDA_REG)
    score = score + jnp.sum(grad_right * grad_right, axis=-1) / (hess_right + LAMBDA_REG)
    score = score - jnp.sum(grad_total * grad_total, axis=-1) / (hess_total + LAMBDA_REG)
    return score * (GAIN_WEIGHT / K)


def channel_rows(gradients, hessian, node_ids):
    channels = jnp.concatenate([gradients, hessian[:, None]], axis=1)
    node_hot = (node_ids[:, None] == jnp.arange(NODES, dtype=jnp.int32)[None, :]).astype(
        jnp.bfloat16
    )
    return (node_hot[:, :, None] * channels[:, None, :]).reshape(node_ids.shape[0], -1)


def column_histograms(columns, weighted):
    row_count, width = columns.shape
    group = math.gcd(width, 32)
    grouped = columns.reshape(row_count, width // group, group).transpose(1, 0, 2)
    levels = jnp.arange(BINS, dtype=jnp.int32)

    def one_group(block):
        bin_hot = (block[:, :, None] == levels).astype(jnp.bfloat16)
        part = jnp.einsum("sfb,sm->fbm", bin_hot, weighted, preferred_element_type=jnp.float32)
        return part.reshape(group, -1)

    return lax.map(one_group, grouped).reshape(width, -1)


def shards(table, sample_rows, gradients, hessian, node_ids, split_feature, split_bin):
    picked = jnp.take(table, sample_rows, axis=0)
    weighted = channel_rows(gradients, hessian, node_ids)
    width = picked.shape[1]
    owned = width // lax.axis_size("dp")
    channel_count = gradients.shape[1] + 1
    terms = column_histograms(picked, weighted)
    mine = lax.psum_scatter(terms, "dp", scatter_dimension=0, tiled=True)
    hist = mine.reshape(owned, BINS, NODES, channel_count)
    left = jnp.cumsum(hist, axis=1)
    total = left[:, -1:]
    best = jnp.max(split_gain(left, total), axis=1).T
    best_gain = lax.all_gather(best, "dp", axis=1, tiled=True)
    feat_index = lax.axis_index("feat")
    node_hot = node_ids[:, None] == jnp.arange(NODES, dtype=jnp.int32)[None, :]
    row_feature = jnp.sum(jnp.where(node_hot, split_feature[None, :], 0), axis=1)
    row_bin = jnp.sum(jnp.where(node_hot, split_bin[None, :], 0), axis=1)
    local_col = row_feature - feat_index * width
    inside = (local_col >= 0) & (local_col < width)
    row_value = jnp.take_along_axis(picked, jnp.clip(local_col, 0, width - 1)[:, None], axis=1)[
        :, 0
    ]
    goes_left = (inside & (row_value <= row_bin)).astype(jnp.bfloat16)
    left_part = jnp.dot(goes_left, weighted, preferred_element_type=jnp.float32)
    all_rows = jnp.ones((weighted.shape[0],), jnp.bfloat16)
    first_flag = jnp.where(feat_index == 0, 1.0, 0.0).astype(jnp.float32)
    total_part = jnp.dot(all_rows, weighted, preferred_element_type=jnp.float32) * first_flag
    left_sum, total_sum = lax.psum((left_part, total_part), ("dp", "feat"))
    left_sum = left_sum.reshape(NODES, channel_count)
    total_sum = total_sum.reshape(NODES, channel_count)
    left_value = -left_sum[:, :K] / (left_sum[:, K:] + LAMBDA_REG)
    right_value = -(total_sum[:, :K] - left_sum[:, :K]) / (
        total_sum[:, K:] - left_sum[:, K:] + LAMBDA_REG
    )
    leaf_values = jnp.stack([left_value, right_value], axis=1).reshape(2 * NODES, K)
    return (best_gain, leaf_values)


def solution(mesh):
    return jax.shard_map(
        shards,
        mesh=mesh,
        in_specs=(P("dp", "feat"), P("dp"), P("dp", None), P("dp"), P("dp"), P(), P()),
        out_specs=(P(None, "feat"), P()),
        check_vma=False,
    )
```

profile of v0, /device:TPU:1, one launch (start us, length us, event | category | flops | bytes accessed | tf_op | source)
XLA Modules:
  0.0 326.2 jit_solution(14134671397800512457)
XLA Ops:
  7.2 0.8 compare_select_fusion.2
  8.7 0.7 constant_dynamic-update-slice_fusion.2
  9.5 1.3 fusion.18
  10.7 1.6 gather_fusion
  12.4 1.4 copy.28
  13.8 2.3 select_bitcast_fusion
  16.1 56.2 %while.11 = (s32[]{:T(128)}, f32[16,32,2176]{2,1,0:T(8,128)}, s32[16,512,32]{1,2,0:T(8,128)}, bf16[512,17]{0,1:T(8,128)(2,1)S(1)}, bf16[512,2]{0,1:T(2,128)(2,1)}, /*index=5*/s32[]{:T(128)}) while((s32[]{:T(128)}, f32[16,32,2176]{2,1,0:T(8,128)}, s32[16,512,32]{1,2,0:T(8,128)}, bf16[512,17]{0,1:T(8,128)(2,1)S(1)}, ...), condition=%wide.region_1.2_spmd.clone, body=%wide.region_0.1_spmd.clone.sunk | while | flops 72369152 | bytes 1748553 | solution.py:49
  16.1 0.8 dynamic-slice_bitcast_fusion.2
  17.7 0.7 fusion.38
  18.9 0.7 constant_dynamic-update-slice_fusion.4
  19.6 0.8 dynamic-slice_bitcast_fusion.2
  22.4 0.7 constant_dynamic-update-slice_fusion.4
  23.1 0.8 dynamic-slice_bitcast_fusion.2
  25.9 0.7 constant_dynamic-update-slice_fusion.4
  26.6 0.8 dynamic-slice_bitcast_fusion.2
  28.2 0.7 fusion.38
  29.4 0.7 constant_dynamic-update-slice_fusion.4
  30.1 0.8 dynamic-slice_bitcast_fusion.2
  32.9 0.7 constant_dynamic-update-slice_fusion.4
  33.7 0.8 dynamic-slice_bitcast_fusion.2
  35.2 0.7 fusion.38
  36.4 0.7 constant_dynamic-update-slice_fusion.4
  37.2 0.8 dynamic-slice_bitcast_fusion.2
  40.7 0.8 dynamic-slice_bitcast_fusion.2
  43.4 0.7 constant_dynamic-update-slice_fusion.4
  44.2 0.8 dynamic-slice_bitcast_fusion.2
  46.9 0.7 constant_dynamic-update-slice_fusion.4
  47.7 0.8 dynamic-slice_bitcast_fusion.2
  50.5 0.7 constant_dynamic-update-slice_fusion.4
  51.2 0.8 dynamic-slice_bitcast_fusion.2
  54.0 0.7 constant_dynamic-update-slice_fusion.4
  54.7 0.8 dynamic-slice_bitcast_fusion.2
  58.2 0.8 dynamic-slice_bitcast_fusion.2
  61.0 0.7 constant_dynamic-update-slice_fusion.4
  61.7 0.8 dynamic-slice_bitcast_fusion.2
  63.3 0.7 fusion.38
  64.5 0.7 constant_dynamic-update-slice_fusion.4
  65.2 0.8 dynamic-slice_bitcast_fusion.2
  68.0 0.7 constant_dynamic-update-slice_fusion.4
  68.7 0.8 dynamic-slice_bitcast_fusion.2
  71.5 0.7 constant_dynamic-update-slice_fusion.4
  73.9 1.2 broadcast_select_fusion
  75.1 7.7 %gather_fusion.1 = s32[512]{0:T(512)S(1)} fusion(s32[512,512]{1,0:T(8,128)} %broadcast_select_fusion, s32[512]{0:T(512)S(1)} %bitcast.61), kind=kCustom, calls=%fused_computation.1 | custom fusion | bytes 8192 | tf_op jit(solution)/shard_map/jit(take_along_axis)/gather | solution.py:71
  83.2 83.4 %all-reduce.1 = (f32[2,17]{1,0:T(2,128)S(1)}, f32[2,17]{1,0:T(2,128)S(1)}) all-reduce(f32[2,17]{1,0:T(2,128)S(1)} %reshape.209, f32[2,17]{1,0:T(2,128)S(1)} %reshape.208), channel_id=1, replica_groups=mesh['dp'=64,'feat'=4] {'dp','feat'}, use_global_device_ids=true, to_apply=%region_11.12 | all-reduce | flops 68 | bytes 544 | tf_op jit(solution)/shard_map/psum | solution.py:79
  168.7 102.5 %all-reduce.4.cloned.1.call-done = f32[512,2176]{1,0:T(8,128)} async-done(((f32[512,2176]{1,0:T(8,128)}), f32[512,2176]{1,0:T(8,128)}) %all-reduce.4.cloned.1.call-update) | async-done | bytes 4456464
  271.2 0.9 constant_dynamic-slice_fusion
  272.1 0.7 reshape.207
  274.5 44.1 %all-gather = f32[64,8,2]{1,2,0:T(2,128)S(1)} all-gather(f32[1,8,2]{1,2,0:T(2,128)S(1)} %bitcast.66), channel_id=1, replica_groups=mesh['dp'=64,'feat'=4] {'dp'}, dimensions={0}, use_global_device_ids=true | all-gather | bytes 4160 | tf_op jit(solution)/shard_map/all_gather | solution.py:64
  (119 shorter events, 35.9 us)
Async XLA Ops:
  7.2 3.6 %copy-start = (s32[1024,512]{1,0:T(8,128)S(1)}, s32[1024,512]{1,0:T(8,128)}, u32[]{:S(2)}) copy-start(s32[1024,512]{1,0:T(8,128)} %param.9) | copy-start | bytes 6291460
  7.2 264.0 %all-reduce.4.cloned.1.call-start = ((), (), s32[]{:S(2)}) async-start(), calls=%async_computation | async-start | bytes 8912896
  8.7 5.0 %copy-start.4 = (pred[512]{0:T(512)(128)(4,1)}, pred[512]{0:T(512)(128)(4,1)S(1)}, u32[]{:S(2)}) copy-start(pred[512]{0:T(512)(128)(4,1)S(1)} %compare_and_fusion.1) | copy-start | bytes 1540
  10.7 3.0 copy-start.6
  12.4 3.7 %copy-start.1 = (s32[512,512]{1,0:T(8,128)}, s32[512,512]{1,0:T(8,128)S(1)}, u32[]{:S(2)}) copy-start(s32[512,512]{1,0:T(8,128)S(1)} %gather_fusion) | copy-start | bytes 3145732
  72.3 0.7 copy-start.3
  72.3 0.7 copy-start.7
  72.3 0.7 copy-start.8
  72.3 1.6 copy-start.2
  72.3 1.6 copy-start.5
  72.3 95.2 %copy-start.9 = (u32[256]{0:T(256)S(1)}, u32[256]{0:T(256)}, u32[]{:S(2)}) copy-start(u32[256]{0:T(256)} %constant.80) | copy-start | bytes 3076
Sparse Core Ops, SparseCore 0:
  72.5 198.7 all-reduce.3
where the time goes:
time: 328 us; the launch traced here: 326 us
  blocking collectives  127 us (39%)
  waiting for transfers between devices  102 us (31%)
  local copies, waits for them, and re-layouts  50 us (15%)
  other arithmetic  19.4 us (6%)
  between operations  14.9 us (5%)
  matrix products  11.8 us (4%)
    unnamed x2, waiting for transfers between devices  102 us
    psum x1, blocking collectives, shards(): left_sum, total_sum = lax.psum((left_part, total_part), ('dp', 'feat'))  83.4 us
    all_gather x1, blocking collectives, shards(): best_gain = lax.all_gather(best, 'dp', axis=1, tiled=True)  44.1 us
    eq x16, local copies, waits for them, and re-layouts, one_group(): bin_hot = (block[:, :, None] == levels).astype(jnp.bfloat16)  13.5 us
    mul x17, other arithmetic, channel_rows(): node_hot[:, :, None] * channels[:, None, :]  11.7 us
    dynamic_update_slice x16, local copies, waits for them, and re-layouts, column_histograms(): return lax.map(one_group, grouped).reshape(width, -1)  11.7 us
    dot_general x16, matrix products, one_group(): jnp.einsum('sfb,sm->fbm', bin_hot, weighted, preferred_element_type=jnp.f...  11.5 us
    broadcast_in_dim x16, local copies, waits for them, and re-layouts, column_histograms(): return lax.map(one_group, grouped).reshape(width, -1)  8.04 us
  transfers between devices with their start and end apart: 1, of which 1 were waited for; matrix products, arithmetic and copies ran while one was open for 4% of the time, Pallas kernels for 0%

commit v1 on v0

v1 whole, which is shorter than its diff:
```python
import functools

import jax
import jax.numpy as jnp
from jax import lax
from jax.experimental import pallas as pl
from jax.experimental.pallas import tpu as pltpu
from jax.sharding import PartitionSpec as P

BINS = 64
K = 16
NODES = 2
LAMBDA_REG = 1.0
GAIN_WEIGHT = 0.01

NX = 8
NZ = 8
NY = 4
S = 512
TAB = 1024
WIDTH = 512
OWN = 8
ROWS = 40
LANES = OWN * BINS
AHEAD = 3
MESH = pl.DeviceIdType.MESH
F32 = jnp.float32
BF16 = jnp.bfloat16


def iota(shape, dim):
    return lax.broadcasted_iota(jnp.int32, shape, dim)


def kernel(
    sf_ref, sb_ref, table_ref, rows_ref, grad_ref, hess_ref, node_ref,
    best_ref, leaf_ref,
    tab, pk, rx, blob, wt, acc, rz, ysend, yrecv, g1, g1r, g2, g2r,
    tab_sem, rx_send, rx_recv, ch_send, ch_recv, rz_send, rz_recv, y_send, y_recv, g_send, g_recv,
):
    d = lax.axis_index("dp")
    y = lax.axis_index("feat")
    z = d // NX
    xd = d % NX

    def xpeer(r):
        return (z * NX + lax.rem(xd + r, NX), y)

    def zpeer(q):
        return (lax.rem(z + q + NZ, NZ) * NX + xd, y)

    def ypeer(r):
        return (d, lax.rem(y + r, NY))

    load = pltpu.make_async_copy(table_ref, tab, tab_sem)
    load.start()

    barrier = pltpu.get_barrier_semaphore()
    for r in range(1, NX):
        pl.semaphore_signal(barrier, inc=1, device_id=xpeer(r), device_id_type=MESH)
    for r in range(1, NZ):
        pl.semaphore_signal(barrier, inc=1, device_id=zpeer(r), device_id_type=MESH)
    for r in range(1, NY):
        pl.semaphore_signal(barrier, inc=1, device_id=ypeer(r), device_id_type=MESH)

    grad_t = grad_ref[...].astype(F32)
    hess = hess_ref[...].astype(F32)
    node = node_ref[...].astype(F32)
    for j in range(S // 128):
        lanes = slice(j * 128, (j + 1) * 128)
        blob[0, j * K:(j + 1) * K, :] = grad_t[:, lanes]
        blob[0, 64 + 2 * j:65 + 2 * j, :] = hess[:, lanes]
        blob[0, 65 + 2 * j:66 + 2 * j, :] = node[:, lanes]

    pl.semaphore_wait(barrier, NX + NZ + NY - 3)

    sib = lax.rem(xd, 2)
    sib_rel = 1 - 2 * sib

    def sibling():
        return (z * NX + xd + sib_rel, y)

    def ch_copy(src_slot, dst_slot, where, k):
        return pltpu.make_async_remote_copy(
            src_ref=blob.at[src_slot], dst_ref=blob.at[dst_slot],
            send_sem=ch_send.at[k], recv_sem=ch_recv.at[dst_slot],
            device_id=where, device_id_type=MESH,
        )

    first = [ch_copy(0, 4 - m, xpeer(2 * m), m) for m in range(1, 4)] + [ch_copy(0, 4, sibling(), 0)]
    for c in first:
        c.start()

    hot = jnp.where(iota((TAB, S), 0) == rows_ref[...], 1.0, 0.0).astype(BF16)
    load.wait()
    for j in range(WIDTH // 128):
        part = tab[:, j * 128:(j + 1) * 128].astype(F32).astype(BF16)
        pk[j * 128:(j + 1) * 128, :] = lax.dot_general(
            part, hot, (((0,), (0,)), ((), ())), preferred_element_type=F32)

    def chunk_z(i):
        half = (i + 1) // 2
        away = jnp.where(i % 2 == 1, 4 - half, 4 + half)
        away = jnp.where(i == 7, 0, away)
        return lax.rem(z + away, NZ)

    def x_copy(i, r):
        peer_x = lax.rem(xd + r, NX)
        row = pl.multiple_of(chunk_z(i) * (NX * OWN) + peer_x * OWN, OWN)
        return pltpu.make_async_remote_copy(
            src_ref=pk.at[pl.ds(row, OWN), :], dst_ref=rx.at[i, NX - r - 1],
            send_sem=rx_send.at[i], recv_sem=rx_recv.at[i],
            device_id=(z * NX + peer_x, y), device_id_type=MESH,
        )

    def start_chunk(i):
        for r in range(1, NX):
            x_copy(i, r).start()

    for i in range(AHEAD):
        start_chunk(i)

    for c in first[:3]:
        c.wait_recv()
    second = [ch_copy(m, 4 + m, sibling(), 3 + m) for m in range(1, 4)]
    for c in second:
        c.start()

    def weights(slot, place):
        for j in range(S // 128):
            g = blob[slot, j * K:(j + 1) * K, :]
            h = blob[slot, 64 + 2 * j:65 + 2 * j, :]
            n = blob[slot, 65 + 2 * j:66 + 2 * j, :]
            at0 = n == 0.0
            at1 = n == 1.0
            rest = jnp.where(iota((16, 128), 0) == 0, jnp.where(at0, h, 0.0),
                             jnp.where(iota((16, 128), 0) == 1, jnp.where(at1, h, 0.0), 0.0))
            full = jnp.concatenate(
                [jnp.where(at0, g, 0.0), jnp.where(at1, g, 0.0), rest], axis=0)
            wt[place, :, j * 128:(j + 1) * 128] = full.astype(BF16)

    weights(0, 0)
    for m in range(1, 4):
        weights(m, 2 * m)

    ind = []
    for n in range(NODES):
        col = sf_ref[n] - y * WIDTH
        inside = jnp.where((col >= 0) & (col < WIDTH), 1.0, 0.0).astype(F32)
        row = pk[pl.ds(jnp.clip(col, 0, WIDTH - 1), 1), :]
        ind.append(jnp.where(row <= sb_ref[n].astype(F32), inside, 0.0))
    ind.append(jnp.full((1, S), jnp.where(y == 0, 1.0, 0.0).astype(F32)))
    ind.append(jnp.zeros((13, S), F32))
    ind = jnp.concatenate(ind, axis=0).astype(BF16)
    leaf_part = lax.dot_general(
        ind, wt[0], (((1,), (1,)), ((), ())), preferred_element_type=F32)
    ysend[...] = jnp.concatenate([leaf_part[:8], jnp.zeros((8, 80), F32)], axis=1)

    def y_copy(r):
        return pltpu.make_async_remote_copy(
            src_ref=ysend, dst_ref=yrecv.at[NY - r - 1],
            send_sem=y_send, recv_sem=y_recv, device_id=ypeer(r), device_id_type=MESH,
        )

    for r in range(1, NY):
        y_copy(r).start()

    first[3].wait_recv()
    for c in second:
        c.wait_recv()
    for m in range(4):
        weights(4 + m, lax.rem(2 * m + sib_rel + NX, NX))

    level = iota((BINS, S), 0).astype(F32).astype(BF16)
    one = jnp.ones((), BF16)
    zero = jnp.zeros((), BF16)

    def below(value):
        return jnp.where(jnp.broadcast_to(value.astype(BF16), (BINS, S)) <= level, one, zero)

    def z_copy(i, target):
        slot = jnp.where(i == 0, 1, i + 2)
        return pltpu.make_async_remote_copy(
            src_ref=acc.at[i], dst_ref=rz.at[slot],
            send_sem=rz_send.at[i], recv_sem=rz_recv.at[slot],
            device_id=target, device_id_type=MESH,
        )

    def chunk(i, carry):
        @pl.when(i + AHEAD < NZ)
        def _():
            start_chunk(i + AHEAD)

        pltpu.make_async_copy(rx.at[i], rx.at[i], rx_recv.at[i]).wait()
        mine = chunk_z(i) * (NX * OWN) + xd * OWN
        total = None
        for r in range(NX):
            hots = []
            for f in range(OWN):
                value = pk[pl.ds(mine + f, 1), :] if r == 0 else rx[i, r - 1, f:f + 1, :]
                hots.append(below(value))
            part = lax.dot_general(
                wt[r], jnp.concatenate(hots, axis=0), (((1,), (1,)), ((), ())),
                preferred_element_type=F32)
            total = part if total is None else total + part
        acc[i] = total[:ROWS]

        @pl.when((i != 0) & (i != 2) & (i != 7))
        def _():
            pltpu.make_async_copy(rz.at[i], rz.at[i], rz_recv.at[i]).wait()
            acc[i] = acc[i] + rz[i]

        @pl.when(i < NZ - 1)
        def _():
            up = (i == 0) | (i % 2 == 1)
            z_copy(i, (lax.rem(z + jnp.where(up, 1, NZ - 1), NZ) * NX + xd, y)).start()

        return carry

    lax.fori_loop(0, NZ, chunk, 0)
    for i in (7, 8):
        pltpu.make_async_copy(rz.at[i], rz.at[i], rz_recv.at[i]).wait()
    left = acc[7] + rz[7] + rz[8]

    total = jnp.broadcast_to(left[:, BINS - 1:BINS], (ROWS, LANES))
    right = total - left
    gains = []
    for n in range(NODES):
        def score(part):
            g = part[n * K:(n + 1) * K]
            h = part[32 + n:33 + n]
            return jnp.sum(g * g, axis=0, keepdims=True) / (h + LAMBDA_REG)
        gains.append((score(left) + score(right) - score(total)) * (GAIN_WEIGHT / K))
    gains = jnp.concatenate(gains + [jnp.zeros((6, LANES), F32)], axis=0)

    lane = iota((8, 128), 1)
    row8 = iota((8, 128), 0)
    base = xd * OWN + lax.rem(z, 2) * 64
    tile = jnp.zeros((8, 128), F32)
    for f in range(OWN):
        top = jnp.max(gains[:, f * BINS:(f + 1) * BINS], axis=1, keepdims=True)
        tile = jnp.where((lane == base + f) & (row8 < 2), top, tile)

    pltpu.make_async_copy(yrecv, yrecv, y_recv).wait()
    leaf_sum = ysend[...] + yrecv[0] + yrecv[1] + yrecv[2]
    leaf_sum = jnp.concatenate([jnp.zeros((2, 128), F32), leaf_sum[:6]], axis=0)
    g1[...] = jnp.where(row8 < 2, tile, leaf_sum)

    def g1_copy(r):
        return pltpu.make_async_remote_copy(
            src_ref=g1, dst_ref=g1r.at[NX - r - 1], send_sem=g_send.at[0], recv_sem=g_recv.at[0],
            device_id=xpeer(r), device_id_type=MESH)

    for r in range(1, NX):
        g1_copy(r).start()
    pltpu.make_async_copy(g1r, g1r, g_recv.at[0]).wait()
    whole = g1[...]
    for r in range(NX - 1):
        whole = whole + g1r[r]
    g2[...] = whole

    def g2_copy(r):
        return pltpu.make_async_remote_copy(
            src_ref=g2, dst_ref=g2r.at[NZ - r - 1], send_sem=g_send.at[1], recv_sem=g_recv.at[1],
            device_id=zpeer(r), device_id_type=MESH)

    for r in range(1, NZ):
        g2_copy(r).start()
    pltpu.make_async_copy(g2r, g2r, g_recv.at[1]).wait()
    tiles = [g2[...]] + [g2r[r] for r in range(NZ - 1)]
    for j in range(WIDTH // 128):
        out = jnp.zeros((8, 128), F32)
        for r in range(NZ):
            here = lax.rem(z + r, NZ) // 2 == j
            out = jnp.where(here, out + tiles[r], out)
        best_ref[:, j * 128:(j + 1) * 128] = out[:2]
    summed = tiles[0]
    for r in range(1, NZ):
        summed = summed + tiles[r]
    tot = summed[4:5]
    for n in range(NODES):
        lft = summed[2 + n:3 + n]
        rgt = tot - lft
        for side, part in enumerate((lft, rgt)):
            g = part[:, n * K:(n + 1) * K]
            h = part[:, 32 + n:33 + n]
            leaf_ref[2 * n + side:2 * n + side + 1, :] = -g / (h + LAMBDA_REG)

    for c in first + second:
        c.wait_send()
    for i in range(NZ):
        pltpu.make_async_copy(rx.at[i], rx.at[i], rx_send.at[i]).wait()
    for i in range(NZ - 1):
        pltpu.make_async_copy(rz.at[i], rz.at[i], rz_send.at[i]).wait()
    pltpu.make_async_copy(yrecv, yrecv, y_send).wait()
    pltpu.make_async_copy(g1r, g1r, g_send.at[0]).wait()
    pltpu.make_async_copy(g2r, g2r, g_send.at[1]).wait()


def shards(table, sample_rows, gradients, hessian, node_ids, split_feature, split_bin):
    vmem = pl.BlockSpec(memory_space=pltpu.VMEM)
    smem = pl.BlockSpec(memory_space=pltpu.SMEM)
    dma = pltpu.SemaphoreType.DMA
    return pl.pallas_call(
        kernel,
        out_shape=(
            jax.ShapeDtypeStruct((NODES, WIDTH), F32),
            jax.ShapeDtypeStruct((2 * NODES, K), F32),
        ),
        in_specs=[smem, smem, pl.BlockSpec(memory_space=pl.ANY), vmem, vmem, vmem, vmem],
        out_specs=(vmem, vmem),
        scratch_shapes=[
            pltpu.VMEM((TAB, WIDTH), jnp.int32),
            pltpu.VMEM((WIDTH, S), F32),
            pltpu.VMEM((NZ, NX - 1, OWN, S), F32),
            pltpu.VMEM((NX, 72, 128), F32),
            pltpu.VMEM((NX, 48, S), BF16),
            pltpu.VMEM((NZ, ROWS, LANES), F32),
            pltpu.VMEM((NZ + 1, ROWS, LANES), F32),
            pltpu.VMEM((8, 128), F32),
            pltpu.VMEM((NY - 1, 8, 128), F32),
            pltpu.VMEM((8, 128), F32),
            pltpu.VMEM((NX - 1, 8, 128), F32),
            pltpu.VMEM((8, 128), F32),
            pltpu.VMEM((NZ - 1, 8, 128), F32),
            dma,
            dma((NZ,)), dma((NZ,)),
            dma((7,)), dma((8,)),
            dma((NZ,)), dma((NZ + 1,)),
            dma, dma,
            dma((2,)), dma((2,)),
        ],
        compiler_params=pltpu.CompilerParams(
            collective_id=0, has_side_effects=True, vmem_limit_bytes=48 * 2**20),
    )(
        split_feature, split_bin, table, sample_rows.reshape(1, S), gradients.T,
        hessian.reshape(1, S), node_ids.reshape(1, S),
    )


def solution(mesh):
    return jax.shard_map(
        shards,
        mesh=mesh,
        in_specs=(P("dp", "feat"), P("dp"), P("dp", None), P("dp"), P("dp"), P(), P()),
        out_specs=(P(None, "feat"), P()),
        check_vma=False,
    )
```

time: 328 us -> 50.2 us (0.15)
  blocking collectives: 127 us -> 0 us
  waiting for transfers between devices: 102 us -> 0 us
  local copies, waits for them, and re-layouts: 50 us -> 6.83 us
  Pallas kernels: 0 us -> 42.5 us
  other arithmetic: 19.4 us -> 0 us
  between operations: 14.9 us -> 0.64 us
  matrix products: 11.8 us -> 0 us
    unnamed x2 -> x0, waiting for transfers between devices: 102 us -> none
    psum x1 -> x0, blocking collectives: 83.4 us -> none  [shards(): left_sum, total_sum = lax.psum((left_part, total_part), ('dp', 'feat'))]
    all_gather x1 -> x0, blocking collectives: 44.1 us -> none  [shards(): best_gain = lax.all_gather(best, 'dp', axis=1, tiled=True)]
    pallas_call x0 -> x1, Pallas kernels: none -> 42.5 us  [shards(): pl.pallas_call(kernel, out_shape=(jax.ShapeDtypeStruct((NODES, WIDTH), F3...]
    eq x16 -> x0, local copies, waits for them, and re-layouts: 13.5 us -> none  [one_group(): bin_hot = (block[:, :, None] == levels).astype(jnp.bfloat16)]
    dot_general x18 -> x0, matrix products: 11.8 us -> none  [the longest x16 11.5 us: one_group(): jnp.einsum('sfb,sm->fbm', bin_hot, weighted, preferred_element_type=jnp.f...]
    mul x17 -> x0, other arithmetic: 11.7 us -> none  [channel_rows(): node_hot[:, :, None] * channels[:, None, :]]
    dynamic_update_slice x16 -> x0, local copies, waits for them, and re-layouts: 11.7 us -> none  [column_histograms(): return lax.map(one_group, grouped).reshape(width, -1)]
  transfers between devices with their start and end apart: 1 -> 0, of which waited for: 1 -> 0; matrix products, arithmetic and copies ran while one was open for 4% -> 0% of each run, Pallas kernels for 0% -> 0%
where the time goes in v1:
time: 50.2 us; the launch traced here: 50 us
  Pallas kernels  42.5 us (85%)
  local copies, waits for them, and re-layouts  6.83 us (14%)
  between operations  0.64 us (1%)
    pallas_call x1, Pallas kernels, shards(): pl.pallas_call(kernel, out_shape=(jax.ShapeDtypeStruct((NODES, WIDTH), F3...  42.5 us
    unnamed x14, local copies, waits for them, and re-layouts  6.15 us

profile of v1, /device:TPU:1, one launch (start us, length us, event | category | flops | bytes accessed | tf_op | source)
XLA Modules:
  0.0 50.0 jit_solution(1465413457576693572)
XLA Ops:
  0.6 0.7 %reshape.14.hess_ref = bf16[1,512]{1,0:T(2,128)(2,1)S(1)} reshape(bf16[512]{0:T(512)(128)(2,1)} %param.10) | data formatting | bytes 2048 | tf_op jit(solution)/shard_map/reshape | solution.py:337
  1.3 0.0 copy-start
  1.3 1.6 %copy-done = s32[1024,512]{1,0:T(8,128)S(1)} copy-done((s32[1024,512]{1,0:T(8,128)S(1)}, s32[1024,512]{1,0:T(8,128)}, u32[]{:S(2)}) %copy-start) | copy-done | bytes 2097176
  2.9 0.0 copy-start.1
  2.9 0.7 %copy-done.1 = bf16[512,16]{0,1:T(8,128)(2,1)S(1)} copy-done((bf16[512,16]{0,1:T(8,128)(2,1)S(1)}, bf16[512,16]{0,1:T(8,128)(2,1)}, u32[]{:S(2)}) %copy-start.1) | copy-done | bytes 16408
  3.6 0.0 copy-start.2
  3.6 0.7 %copy-done.2 = s32[512]{0:T(512)S(1)} copy-done((s32[512]{0:T(512)S(1)}, s32[512]{0:T(512)}, u32[]{:S(2)}) %copy-start.2) | copy-done | bytes 2072
  4.3 0.0 copy-start.3
  4.3 0.7 %copy-done.3 = s32[512]{0:T(512)S(1)} copy-done((s32[512]{0:T(512)S(1)}, s32[512]{0:T(512)}, u32[]{:S(2)}) %copy-start.3) | copy-done | bytes 2072
  5.0 0.0 copy-start.4
  5.0 0.7 %copy-done.4 = s32[2]{0:T(128)S(1)} copy-done((s32[2]{0:T(128)S(1)}, s32[2]{0:T(128)}, u32[]{:S(2)}) %copy-start.4) | copy-done | bytes 32
  5.6 0.0 copy-start.5
  5.6 0.7 %copy-done.5 = s32[2]{0:T(128)S(1)} copy-done((s32[2]{0:T(128)S(1)}, s32[2]{0:T(128)}, u32[]{:S(2)}) %copy-start.5) | copy-done | bytes 32
  6.3 42.5 %shard_map.86 = (f32[2,512]{1,0:T(2,128)S(1)}, f32[4,16]{1,0:T(4,128)S(1)}) custom-call(s32[2]{0:T(128)S(1)} %copy-done.4, s32[2]{0:T(128)S(1)} %copy-done.5, s32[1024,512]{1,0:T(8,128)S(1)} %copy-done, s32[1,512]{1,0:T(1,128)S(1)} %bitcast.4, bf16[16,512]{1,0:T(8,128)(2,1)S(1)} %bitcast.3, bf16[1,512]{1,0:T(2,128)(2,1)S(1)} %reshape.14.hess_ref, ...), custom_call_target="tpu_custom_call" | custom-call | tf_op jit(solution)/shard_map/pallas_call | solution.py:304
  48.8 0.6 %copy.11 = f32[2,512]{1,0:T(2,128)} copy(f32[2,512]{1,0:T(2,128)S(1)} %get-tuple-element.4) | data formatting | bytes 8192
  49.4 0.6 %copy.12 = f32[4,16]{1,0:T(4,128)} copy(f32[4,16]{1,0:T(4,128)S(1)} %get-tuple-element.5) | data formatting | bytes 512
Async XLA Ops:
  1.3 1.6 %copy-start = (s32[1024,512]{1,0:T(8,128)S(1)}, s32[1024,512]{1,0:T(8,128)}, u32[]{:S(2)}) copy-start(s32[1024,512]{1,0:T(8,128)} %table_ref.1) | copy-start | bytes 6291460
  2.9 0.7 %copy-start.1 = (bf16[512,16]{0,1:T(8,128)(2,1)S(1)}, bf16[512,16]{0,1:T(8,128)(2,1)}, u32[]{:S(2)}) copy-start(bf16[512,16]{0,1:T(8,128)(2,1)} %param.9) | copy-start | bytes 49156
  3.6 0.7 %copy-start.2 = (s32[512]{0:T(512)S(1)}, s32[512]{0:T(512)}, u32[]{:S(2)}) copy-start(s32[512]{0:T(512)} %param.8) | copy-start | bytes 6148
  4.3 0.7 %copy-start.3 = (s32[512]{0:T(512)S(1)}, s32[512]{0:T(512)}, u32[]{:S(2)}) copy-start(s32[512]{0:T(512)} %param.11) | copy-start | bytes 6148
  5.0 0.7 %copy-start.4 = (s32[2]{0:T(128)S(1)}, s32[2]{0:T(128)}, u32[]{:S(2)}) copy-start(s32[2]{0:T(128)} %sf_ref.1) | copy-start | bytes 28
  5.6 0.7 %copy-start.5 = (s32[2]{0:T(128)S(1)}, s32[2]{0:T(128)}, u32[]{:S(2)}) copy-start(s32[2]{0:T(128)} %sb_ref.1) | copy-start | bytes 28

commit v2 on v0

v2 whole, which is shorter than its diff:
```python
import jax
import jax.numpy as jnp
from jax import lax
from jax.experimental import pallas as pl
from jax.experimental.pallas import tpu as pltpu
from jax.sharding import PartitionSpec as P

BINS = 64
K = 16
NODES = 2
LAMBDA_REG = 1.0
GAIN_WEIGHT = 0.01

NX = 8
NZ = 8
NY = 4
S = 512
TAB = 1024
WIDTH = 512
OWN = 8
COLS = WIDTH // 128
WROWS = 48
HROWS = COLS * 32 + 8
FAR = (4, 3, 5, 2, 6, 1, 7, 0)
MESH = pl.DeviceIdType.MESH
F32 = jnp.float32
BF16 = jnp.bfloat16


def iota(shape, dim):
    return lax.broadcasted_iota(jnp.int32, shape, dim)


def choose(i, values):
    out = values[-1]
    for k in range(len(values) - 2, -1, -1):
        out = jnp.where(i == k, values[k], out)
    return out


def nt(a, b):
    return lax.dot_general(a, b, (((1,), (1,)), ((), ())), preferred_element_type=F32)


def kernel(
    sf_hbm, sb_hbm, table_hbm, rows_hbm, grad_hbm, hess_hbm, node_hbm,
    best_ref, leaf_ref,
    sf, sb, tab, rows_v, grad_v, hess_v, node_v, pk, rx, blob, wt, acc, zs, rz,
    lf, lfy, lfx, lfz, fin, fin_own,
    in_sem, tab_sem, rx_send, rx_recv, sib_send, sib_recv, ch_send, ch_recv, rz_send, rz_recv,
    l_send, l_recv, f_send, f_recv,
):
    d = lax.axis_index("dp")
    y = lax.axis_index("feat")
    z = d // NX
    xd = d % NX
    core = xd % 2
    sib_rel = 1 - 2 * core

    def xpeer(r):
        return (z * NX + lax.rem(xd + r, NX), y)

    def zpeer(q):
        return (lax.rem(z + q, NZ) * NX + xd, y)

    def ypeer(r):
        return (d, lax.rem(y + r, NY))

    sibling = (d + sib_rel, y)

    ins = [
        pltpu.make_async_copy(src, dst, in_sem.at[k])
        for k, (src, dst) in enumerate((
            (rows_hbm, rows_v), (grad_hbm, grad_v), (hess_hbm, hess_v), (node_hbm, node_v),
            (sf_hbm, sf), (sb_hbm, sb)))
    ]
    ins[0].start()
    first_col = lax.rem(z // 2 + 2, COLS)

    def col(j):
        return pl.multiple_of(lax.rem(first_col + j, COLS) * 128, 128)

    loads = [
        pltpu.make_async_copy(
            table_hbm.at[:, pl.ds(col(j), 128)], tab.at[j], tab_sem.at[j])
        for j in range(COLS)
    ]
    for c in loads:
        c.start()
    for c in ins[1:]:
        c.start()

    barrier = pltpu.get_barrier_semaphore()
    for r in FAR[:-1]:
        pl.semaphore_signal(barrier, inc=1, device_id=zpeer(r), device_id_type=MESH)
    for r in range(1, NX):
        pl.semaphore_signal(barrier, inc=1, device_id=xpeer(r), device_id_type=MESH)
    for r in range(1, NY):
        pl.semaphore_signal(barrier, inc=1, device_id=ypeer(r), device_id_type=MESH)

    for c in ins[1:]:
        c.wait()
    for j in range(COLS):
        lanes = slice(j * 128, (j + 1) * 128)
        blob[0, j * K:(j + 1) * K, :] = grad_v[:, lanes].astype(F32)
        blob[0, 64 + 2 * j:65 + 2 * j, :] = hess_v[j:j + 1, :].astype(F32)
        blob[0, 65 + 2 * j:66 + 2 * j, :] = node_v[:, lanes].astype(F32)

    ins[0].wait()
    hot = jnp.where(iota((TAB, S), 0) == rows_v[...], 1.0, 0.0).astype(BF16)

    for j in range(COLS):
        loads[j].wait()
        part = tab[j].astype(F32).astype(BF16)
        pk[pl.ds(col(j), 128), :] = lax.dot_general(
            part, hot, (((0,), (0,)), ((), ())), preferred_element_type=F32)

    pl.semaphore_wait(barrier, NX + NZ + NY - 3)

    def ch_copy(src_slot, dst_slot, where, k):
        return pltpu.make_async_remote_copy(
            src_ref=blob.at[src_slot], dst_ref=blob.at[dst_slot],
            send_sem=ch_send.at[k], recv_sem=ch_recv.at[dst_slot],
            device_id=where, device_id_type=MESH,
        )

    first = [ch_copy(0, 4 - m, xpeer(2 * m), m) for m in range(1, 4)] + [ch_copy(0, 4, sibling, 0)]
    for c in first:
        c.start()

    def chunk_z(i):
        return lax.rem(z + choose(i, (3, 5, 4, 2, 6, 1, 7, 0)), NZ)

    def x_copy(i, m, other):
        peer_x = lax.rem(xd + 2 * m + NX, NX)
        peer_x = jnp.where(other, peer_x + sib_rel, peer_x) if other else peer_x
        row = pl.multiple_of(chunk_z(i) * (NX * OWN) + peer_x * OWN, OWN)
        if m == 0:
            send, recv, slot = sib_send, sib_recv, 0
        else:
            send, recv, slot = rx_send.at[i], rx_recv.at[i], (3 if other else 0) + 4 - m
        return pltpu.make_async_remote_copy(
            src_ref=pk.at[pl.ds(row, OWN), :],
            dst_ref=rx.at[slot, i],
            send_sem=send, recv_sem=recv,
            device_id=(z * NX + peer_x, y), device_id_type=MESH,
        )

    def weights(slot, place):
        for j in range(COLS):
            g = blob[slot, j * K:(j + 1) * K, :]
            h = blob[slot, 64 + 2 * j:65 + 2 * j, :]
            n = blob[slot, 65 + 2 * j:66 + 2 * j, :]
            at0 = n == 0.0
            at1 = n == 1.0
            rest = jnp.where(iota((16, 128), 0) == 0, jnp.where(at0, h, 0.0),
                             jnp.where(iota((16, 128), 0) == 1, jnp.where(at1, h, 0.0), 0.0))
            full = jnp.concatenate(
                [jnp.where(at0, g, 0.0), jnp.where(at1, g, 0.0), rest], axis=0)
            wt[place, :, j * 128:(j + 1) * 128] = full.astype(BF16)

    level = iota((BINS, S), 0).astype(F32).astype(BF16)
    one = jnp.ones((), BF16)
    zero = jnp.zeros((), BF16)

    def below(value):
        return jnp.where(jnp.broadcast_to(value.astype(BF16), (BINS, S)) <= level, one, zero)

    def product(place, values):
        return nt(wt[place], jnp.concatenate([below(v) for v in values], axis=0))

    weights(0, 0)

    def own_chunk(i, carry):
        for m in (2, 1, 3):
            x_copy(i, m, False).start()
            x_copy(i, m, True).start()
        x_copy(i, 0, True).start()
        mine = chunk_z(i) * (NX * OWN) + xd * OWN
        acc[i] = product(0, [pk[pl.ds(mine + f, 1), :] for f in range(OWN)])
        return carry

    lax.fori_loop(0, NZ, own_chunk, 0)

    sides = []
    for n in range(NODES):
        at = sf[n] - y * WIDTH
        inside = jnp.where((at >= 0) & (at < WIDTH), 1.0, 0.0).astype(F32)
        row = pk[pl.ds(jnp.clip(at, 0, WIDTH - 1), 1), :]
        sides.append(jnp.where(row <= sb[n].astype(F32), inside, 0.0))
    ind = jnp.concatenate([
        jnp.where(node_v[...] == 0, sides[0], sides[1]),
        jnp.full((1, S), jnp.where(y == 0, 1.0, 0.0).astype(F32)),
        jnp.zeros((14, S), F32)], axis=0).astype(BF16)
    part = nt(ind, wt[0])
    gap = jnp.zeros((1, 64 - WROWS), F32)
    lf[0] = jnp.concatenate([part[:1], gap, part[1:2], gap], axis=1)

    def l_copy(stage, dst, where):
        return pltpu.make_async_remote_copy(
            src_ref=lf.at[stage], dst_ref=dst, send_sem=l_send.at[stage], recv_sem=l_recv.at[stage],
            device_id=where, device_id_type=MESH)

    for r in range(1, NY):
        l_copy(0, lfy.at[NY - r - 1], ypeer(r)).start()

    for c in first[:3]:
        c.wait_recv()
    second = [ch_copy(m, 4 + m, sibling, 3 + m) for m in range(1, 4)]
    for c in second:
        c.start()

    first[3].wait_recv()
    weights(4, 4)
    pltpu.make_async_copy(rx.at[0], rx.at[0], sib_recv).wait()

    def sib_chunk(i, carry):
        acc[i] += product(4, [rx[0, i, f:f + 1, :] for f in range(OWN)])
        return carry

    lax.fori_loop(0, NZ, sib_chunk, 0)

    for m in range(1, 4):
        weights(m, m)
    for c in second:
        c.wait_recv()
    for m in range(5, 8):
        weights(m, m)

    def z_copy(i):
        dz = choose(i, (1, 7, 4, 2, 6, 1, 7))
        return pltpu.make_async_remote_copy(
            src_ref=zs.at[i], dst_ref=rz.at[i],
            send_sem=rz_send.at[i], recv_sem=rz_recv.at[i],
            device_id=(lax.rem(z + dz, NZ) * NX + xd, y), device_id_type=MESH,
        )

    def chunk(i, carry):
        six = rx.at[pl.ds(1, 6), 0]
        pltpu.make_async_copy(six, six, rx_recv.at[i]).wait()
        total = acc[i]
        for slot in range(1, 7):
            place = slot if slot < 4 else slot + 1
            total = total + product(place, [rx[slot, i, f:f + 1, :] for f in range(OWN)])
        for j in range(COLS):
            lanes = slice(j * 128, (j + 1) * 128)
            zs[i, j * 32:(j + 1) * 32, :] = total[:32, lanes]
            zs[i, 128 + 2 * j:130 + 2 * j, :] = total[32:34, lanes]

        @pl.when((i == 3) | (i == 4))
        def _():
            pltpu.make_async_copy(rz.at[i - 3], rz.at[i - 3], rz_recv.at[i - 3]).wait()
            zs[i] = zs[i] + rz[i - 3]

        @pl.when(i < NZ - 1)
        def _():
            z_copy(i).start()

        @pl.when(i == 1)
        def _():
            pltpu.make_async_copy(lfy, lfy, l_recv.at[0]).wait()
            lf[1] = lf[0] + lfy[0] + lfy[1] + lfy[2]
            for r in range(1, NX):
                l_copy(1, lfx.at[NX - r - 1], xpeer(r)).start()

        @pl.when(i == 4)
        def _():
            pltpu.make_async_copy(lfx, lfx, l_recv.at[1]).wait()
            s = lf[1]
            for r in range(NX - 1):
                s = s + lfx[r]
            lf[2] = s
            for r in range(1, NZ):
                l_copy(2, lfz.at[NZ - r - 1], zpeer(r)).start()

        return carry

    lax.fori_loop(0, NZ, chunk, 0)
    pltpu.make_async_copy(lfz, lfz, l_recv.at[2]).wait()
    for i in range(2, 7):
        pltpu.make_async_copy(rz.at[i], rz.at[i], rz_recv.at[i]).wait()
    left = zs[7] + rz[2] + rz[3] + rz[4] + rz[5] + rz[6]

    tot_g = jnp.broadcast_to(left[:32, BINS - 1:BINS], (32, 128))
    tot_h = jnp.broadcast_to(left[128:130, BINS - 1:BINS], (2, 128))

    def score(g, h):
        return jnp.sum(g * g, axis=0, keepdims=True) / (h + LAMBDA_REG)

    gains = []
    for j in range(COLS):
        for n in range(NODES):
            gl = left[j * 32 + n * K:j * 32 + (n + 1) * K]
            hl = left[128 + 2 * j + n:129 + 2 * j + n]
            gt = tot_g[n * K:(n + 1) * K]
            ht = tot_h[n:n + 1]
            gains.append(score(gl, hl) + score(gt - gl, ht - hl) - score(gt, ht))
    gains = jnp.concatenate(gains, axis=0) * (GAIN_WEIGHT / K)
    lane = iota((8, 128), 1)
    row8 = iota((8, 128), 0)
    low = jnp.max(jnp.where(lane < BINS, gains, -jnp.inf), axis=1, keepdims=True)
    high = jnp.max(jnp.where(lane >= BINS, gains, -jnp.inf), axis=1, keepdims=True)
    home = lax.rem(row8 + z, 2) * 64 + xd * OWN + (row8 // 2) * 2
    mine = jnp.where(lane == home, low, jnp.where(lane == home + 1, high, 0.0))
    mine = jnp.sum(mine, axis=0, keepdims=True)
    fin_own[...] = mine
    fin[d] = mine

    def f_copy(q, r):
        return pltpu.make_async_remote_copy(
            src_ref=fin_own, dst_ref=fin.at[d], send_sem=f_send, recv_sem=f_recv,
            device_id=(lax.rem(z + q, NZ) * NX + lax.rem(xd + r, NX), y), device_id_type=MESH)

    pairs = [(q, r) for q in FAR for r in FAR if q or r]
    for q, r in pairs:
        f_copy(q, r).start()

    s = lf[2]
    for r in range(NZ - 1):
        s = s + lfz[r]
    for n in range(NODES):
        tot = s[:, 64:128]
        lft = s[:, 0:64]
        for side, part in enumerate((lft, tot - lft)):
            g = part[:, n * K:(n + 1) * K]
            h = part[:, 32 + n:33 + n]
            leaf_ref[2 * n + side:2 * n + side + 1, :] = -g / (h + LAMBDA_REG)

    for c in first + second:
        c.wait_send()
    six = rx.at[pl.ds(1, 6), 0]
    for i in range(NZ):
        pltpu.make_async_copy(six, six, rx_send.at[i]).wait()
    pltpu.make_async_copy(rx.at[0], rx.at[0], sib_send).wait()
    for i in range(NZ - 1):
        pltpu.make_async_copy(rz.at[i], rz.at[i], rz_send.at[i]).wait()
    pltpu.make_async_copy(lfy, lfy, l_send.at[0]).wait()
    pltpu.make_async_copy(lfx, lfx, l_send.at[1]).wait()
    pltpu.make_async_copy(lfz, lfz, l_send.at[2]).wait()

    others = fin.at[pl.ds(0, NX * NZ - 1)]
    pltpu.make_async_copy(others, others, f_recv).wait()
    lane1 = iota((1, 128), 1)
    for j in range(COLS):
        pair = []
        for q in (2 * j, 2 * j + 1):
            v = fin[q * NX]
            for r in range(1, NX):
                v = v + fin[q * NX + r]
            pair.append(v)
        best_ref[0:1, j * 128:(j + 1) * 128] = jnp.where(lane1 < 64, pair[0], pair[1])
        best_ref[1:2, j * 128:(j + 1) * 128] = pltpu.roll(
            jnp.where(lane1 < 64, pair[1], pair[0]), 64, axis=1)
    pltpu.make_async_copy(others, others, f_send).wait()


def shards(table, sample_rows, gradients, hessian, node_ids, split_feature, split_bin):
    vmem = pl.BlockSpec(memory_space=pltpu.VMEM)
    hbm = pl.BlockSpec(memory_space=pltpu.HBM)
    dma = pltpu.SemaphoreType.DMA
    row = pltpu.VMEM((1, 128), F32)
    return pl.pallas_call(
        kernel,
        out_shape=(
            jax.ShapeDtypeStruct((NODES, WIDTH), F32),
            jax.ShapeDtypeStruct((2 * NODES, K), F32),
        ),
        in_specs=[hbm] * 7,
        out_specs=(vmem, vmem),
        scratch_shapes=[
            pltpu.SMEM((NODES,), jnp.int32),
            pltpu.SMEM((NODES,), jnp.int32),
            pltpu.VMEM((COLS, TAB, 128), jnp.int32),
            pltpu.VMEM((1, S), jnp.int32),
            pltpu.VMEM((K, S), BF16),
            pltpu.VMEM((COLS, 128), BF16),
            pltpu.VMEM((1, S), jnp.int32),
            pltpu.VMEM((WIDTH, S), F32),
            pltpu.VMEM((NX - 1, NZ, OWN, S), F32),
            pltpu.VMEM((NX, 72, 128), F32),
            pltpu.VMEM((NX, WROWS, S), BF16),
            pltpu.VMEM((NZ, WROWS, OWN * BINS), F32),
            pltpu.VMEM((NZ, HROWS, 128), F32),
            pltpu.VMEM((NZ - 1, HROWS, 128), F32),
            pltpu.VMEM((3, 1, 128), F32),
            pltpu.VMEM((NY - 1, 1, 128), F32),
            pltpu.VMEM((NX - 1, 1, 128), F32),
            pltpu.VMEM((NZ - 1, 1, 128), F32),
            pltpu.VMEM((NX * NZ, 1, 128), F32),
            row,
            dma((6,)), dma((COLS,)),
            dma((NZ,)), dma((NZ,)),
            dma, dma,
            dma((7,)), dma((8,)),
            dma((NZ - 1,)), dma((NZ - 1,)),
            dma((3,)), dma((3,)),
            dma, dma,
        ],
        compiler_params=pltpu.CompilerParams(
            collective_id=0, has_side_effects=True, vmem_limit_bytes=60 * 2**20),
    )(
        split_feature, split_bin, table, sample_rows.reshape(1, S), gradients.T,
        hessian.reshape(COLS, 128), node_ids.reshape(1, S),
    )


def solution(mesh):
    return jax.shard_map(
        shards,
        mesh=mesh,
        in_specs=(P("dp", "feat"), P("dp"), P("dp", None), P("dp"), P("dp"), P(), P()),
        out_specs=(P(None, "feat"), P()),
        check_vma=False,
    )
```

time: 328 us -> 40.9 us (0.12)
  blocking collectives: 127 us -> 0 us
  waiting for transfers between devices: 102 us -> 0 us
  local copies, waits for them, and re-layouts: 50 us -> 2.5 us
  Pallas kernels: 0 us -> 37.6 us
  other arithmetic: 19.4 us -> 0 us
  between operations: 14.9 us -> 0.64 us
  matrix products: 11.8 us -> 0 us
    unnamed x2 -> x0, waiting for transfers between devices: 102 us -> none
    psum x1 -> x0, blocking collectives: 83.4 us -> none  [shards(): left_sum, total_sum = lax.psum((left_part, total_part), ('dp', 'feat'))]
    all_gather x1 -> x0, blocking collectives: 44.1 us -> none  [shards(): best_gain = lax.all_gather(best, 'dp', axis=1, tiled=True)]
    pallas_call x0 -> x1, Pallas kernels: none -> 37.6 us  [shards(): pl.pallas_call(kernel, out_shape=(jax.ShapeDtypeStruct((NODES, WIDTH), F3...]
    eq x16 -> x0, local copies, waits for them, and re-layouts: 13.5 us -> none  [one_group(): bin_hot = (block[:, :, None] == levels).astype(jnp.bfloat16)]
    dot_general x18 -> x0, matrix products: 11.8 us -> none  [the longest x16 11.5 us: one_group(): jnp.einsum('sfb,sm->fbm', bin_hot, weighted, preferred_element_type=jnp.f...]
    mul x17 -> x0, other arithmetic: 11.7 us -> none  [channel_rows(): node_hot[:, :, None] * channels[:, None, :]]
    dynamic_update_slice x16 -> x0, local copies, waits for them, and re-layouts: 11.7 us -> none  [column_histograms(): return lax.map(one_group, grouped).reshape(width, -1)]
  transfers between devices with their start and end apart: 1 -> 0, of which waited for: 1 -> 0; matrix products, arithmetic and copies ran while one was open for 4% -> 0% of each run, Pallas kernels for 0% -> 0%
where the time goes in v2:
time: 40.9 us; the launch traced here: 40.8 us
  Pallas kernels  37.6 us (92%)
  local copies, waits for them, and re-layouts  2.5 us (6%)
  between operations  0.64 us (2%)
    pallas_call x1, Pallas kernels, shards(): pl.pallas_call(kernel, out_shape=(jax.ShapeDtypeStruct((NODES, WIDTH), F3...  37.6 us
    unnamed x2, local copies, waits for them, and re-layouts  2.5 us

profile of v2, /device:TPU:1, one launch (start us, length us, event | category | flops | bytes accessed | tf_op | source)
XLA Modules:
  0.0 40.8 jit_solution(13427063819060926124)
XLA Ops:
  0.6 37.6 %shard_map.86 = (f32[2,512]{1,0:T(2,128)}, f32[4,16]{1,0:T(4,128)}) custom-call(s32[2]{0:T(128)} %sf_hbm.1, s32[2]{0:T(128)} %sb_hbm.1, s32[1024,512]{1,0:T(8,128)} %table_hbm.1, s32[1,512]{1,0:T(1,128)} %bitcast.5, bf16[16,512]{1,0:T(8,128)(2,1)} %bitcast.4, bf16[4,128]{1,0:T(4,128)(2,1)} %bitcast.7, s32[1,512]{1,0:T(1,128)} %bitcast.6), custom_call_target="tpu_custom_call" | custom-call | tf_op jit(solution)/shard_map/pallas_call | solution.py:362
  38.3 1.3 %copy.11 = f32[2,512]{1,0:T(2,128)} copy(f32[2,512]{1,0:T(2,128)} %get-tuple-element.4) | data formatting | bytes 8192
  39.5 1.2 %copy.12 = f32[4,16]{1,0:T(4,128)} copy(f32[4,16]{1,0:T(4,128)} %get-tuple-element.5) | data formatting | bytes 512

commit v3 on v2

--- a/solution.py
+++ b/solution.py
@@ -21,6 +21,7 @@
 COLS = WIDTH // 128
 WROWS = 48
 HROWS = COLS * 32 + 8
+AHEAD = 3
 FAR = (4, 3, 5, 2, 6, 1, 7, 0)
 MESH = pl.DeviceIdType.MESH
 F32 = jnp.float32
@@ -44,11 +45,11 @@
 
 def kernel(
     sf_hbm, sb_hbm, table_hbm, rows_hbm, grad_hbm, hess_hbm, node_hbm,
-    best_ref, leaf_ref,
+    fin, leaf_sum,
     sf, sb, tab, rows_v, grad_v, hess_v, node_v, pk, rx, blob, wt, acc, zs, rz,
-    lf, lfy, lfx, lfz, fin, fin_own,
+    lf, lfy, lfx, lfz, fin_own, leaf_v,
     in_sem, tab_sem, rx_send, rx_recv, sib_send, sib_recv, ch_send, ch_recv, rz_send, rz_recv,
-    l_send, l_recv, f_send, f_recv,
+    l_send, l_recv, f_send, f_recv, out_sem, hello,
 ):
     d = lax.axis_index("dp")
     y = lax.axis_index("feat")
@@ -56,6 +57,7 @@
     xd = d % NX
     core = xd % 2
     sib_rel = 1 - 2 * core
+    turn = 1 - 2 * lax.rem(z, 2)
 
     def xpeer(r):
         return (z * NX + lax.rem(xd + r, NX), y)
@@ -75,10 +77,10 @@
             (sf_hbm, sf), (sb_hbm, sb)))
     ]
     ins[0].start()
-    first_col = lax.rem(z // 2 + 2, COLS)
 
     def col(j):
-        return pl.multiple_of(lax.rem(first_col + j, COLS) * 128, 128)
+        ahead = (2, 2 - turn, 2 + turn, 0)[j]
+        return pl.multiple_of(lax.rem(z // 2 + ahead, COLS) * 128, 128)
 
     loads = [
         pltpu.make_async_copy(
@@ -91,12 +93,19 @@
         c.start()
 
     barrier = pltpu.get_barrier_semaphore()
-    for r in FAR[:-1]:
+    for r in (1, NZ - 1):
         pl.semaphore_signal(barrier, inc=1, device_id=zpeer(r), device_id_type=MESH)
     for r in range(1, NX):
         pl.semaphore_signal(barrier, inc=1, device_id=xpeer(r), device_id_type=MESH)
     for r in range(1, NY):
         pl.semaphore_signal(barrier, inc=1, device_id=ypeer(r), device_id_type=MESH)
+
+    def greet(k):
+        for r in (1, NZ - 1):
+            pl.semaphore_signal(hello.at[k], inc=1, device_id=zpeer(r), device_id_type=MESH)
+
+    def greeted(k):
+        pl.semaphore_wait(hello.at[k], 2)
 
     for c in ins[1:]:
         c.wait()
@@ -109,14 +118,6 @@
     ins[0].wait()
     hot = jnp.where(iota((TAB, S), 0) == rows_v[...], 1.0, 0.0).astype(BF16)
 
-    for j in range(COLS):
-        loads[j].wait()
-        part = tab[j].astype(F32).astype(BF16)
-        pk[pl.ds(col(j), 128), :] = lax.dot_general(
-            part, hot, (((0,), (0,)), ((), ())), preferred_element_type=F32)
-
-    pl.semaphore_wait(barrier, NX + NZ + NY - 3)
-
     def ch_copy(src_slot, dst_slot, where, k):
         return pltpu.make_async_remote_copy(
             src_ref=blob.at[src_slot], dst_ref=blob.at[dst_slot],
@@ -125,11 +126,9 @@
         )
 
     first = [ch_copy(0, 4 - m, xpeer(2 * m), m) for m in range(1, 4)] + [ch_copy(0, 4, sibling, 0)]
-    for c in first:
-        c.start()
 
     def chunk_z(i):
-        return lax.rem(z + choose(i, (3, 5, 4, 2, 6, 1, 7, 0)), NZ)
+        return lax.rem(z + NZ + choose(i, (4, -3 * turn, 3 * turn, 2 * turn, -2 * turn, -turn, turn, 0)), NZ)
 
     def x_copy(i, m, other):
         peer_x = lax.rem(xd + 2 * m + NX, NX)
@@ -146,6 +145,30 @@
             device_id=(z * NX + peer_x, y), device_id_type=MESH,
         )
 
+    def start_chunk(i):
+        for m in (2, 1, 3):
+            x_copy(i, m, False).start()
+            x_copy(i, m, True).start()
+
+    for j in range(COLS):
+        loads[j].wait()
+        part = tab[j].astype(F32).astype(BF16)
+        pk[pl.ds(col(j), 128), :] = lax.dot_general(
+            part, hot, (((0,), (0,)), ((), ())), preferred_element_type=F32)
+        if j == 0:
+            pl.semaphore_wait(barrier, NX + NY)
+            for c in first:
+                c.start()
+        for i in (2 * j, 2 * j + 1):
+            if i < AHEAD:
+                start_chunk(i)
+            x_copy(i, 0, True).start()
+        if j == 0:
+            greet(0)
+        if j == 2:
+            greeted(0)
+            greet(1)
+
     def weights(slot, place):
         for j in range(COLS):
             g = blob[slot, j * K:(j + 1) * K, :]
@@ -172,15 +195,14 @@
     weights(0, 0)
 
     def own_chunk(i, carry):
-        for m in (2, 1, 3):
-            x_copy(i, m, False).start()
-            x_copy(i, m, True).start()
-        x_copy(i, 0, True).start()
         mine = chunk_z(i) * (NX * OWN) + xd * OWN
         acc[i] = product(0, [pk[pl.ds(mine + f, 1), :] for f in range(OWN)])
         return carry
 
     lax.fori_loop(0, NZ, own_chunk, 0)
+
+    greeted(1)
+    greet(2)
 
     sides = []
     for n in range(NODES):
@@ -226,16 +248,21 @@
         c.wait_recv()
     for m in range(5, 8):
         weights(m, m)
+    greeted(2)
 
     def z_copy(i):
-        dz = choose(i, (1, 7, 4, 2, 6, 1, 7))
+        dz = choose(i, (-turn, -turn, turn, 2 * turn, -2 * turn, -turn, turn))
         return pltpu.make_async_remote_copy(
             src_ref=zs.at[i], dst_ref=rz.at[i],
             send_sem=rz_send.at[i], recv_sem=rz_recv.at[i],
-            device_id=(lax.rem(z + dz, NZ) * NX + xd, y), device_id_type=MESH,
+            device_id=(lax.rem(z + NZ + dz, NZ) * NX + xd, y), device_id_type=MESH,
         )
 
     def chunk(i, carry):
+        @pl.when(i + AHEAD < NZ)
+        def _():
+            start_chunk(i + AHEAD)
+
         six = rx.at[pl.ds(1, 6), 0]
         pltpu.make_async_copy(six, six, rx_recv.at[i]).wait()
         total = acc[i]
@@ -247,14 +274,16 @@
             zs[i, j * 32:(j + 1) * 32, :] = total[:32, lanes]
             zs[i, 128 + 2 * j:130 + 2 * j, :] = total[32:34, lanes]
 
-        @pl.when((i == 3) | (i == 4))
-        def _():
-            pltpu.make_async_copy(rz.at[i - 3], rz.at[i - 3], rz_recv.at[i - 3]).wait()
-            zs[i] = zs[i] + rz[i - 3]
-
-        @pl.when(i < NZ - 1)
+        @pl.when((i < 2) | (i == 5) | (i == 6))
         def _():
             z_copy(i).start()
+
+        @pl.when((i == 3) | (i == 4) | (i == 6))
+        def _():
+            c = jnp.where(i == 6, 4, i - 1)
+            pltpu.make_async_copy(rz.at[c - 2], rz.at[c - 2], rz_recv.at[c - 2]).wait()
+            zs[c] = zs[c] + rz[c - 2]
+            z_copy(c).start()
 
         @pl.when(i == 1)
         def _():
@@ -277,9 +306,9 @@
 
     lax.fori_loop(0, NZ, chunk, 0)
     pltpu.make_async_copy(lfz, lfz, l_recv.at[2]).wait()
-    for i in range(2, 7):
+    for i in (3, 4, 5, 6):
         pltpu.make_async_copy(rz.at[i], rz.at[i], rz_recv.at[i]).wait()
-    left = zs[7] + rz[2] + rz[3] + rz[4] + rz[5] + rz[6]
+    left = zs[7] + rz[3] + rz[4] + rz[5] + rz[6]
 
     tot_g = jnp.broadcast_to(left[:32, BINS - 1:BINS], (32, 128))
     tot_h = jnp.broadcast_to(left[128:130, BINS - 1:BINS], (2, 128))
@@ -304,27 +333,28 @@
     mine = jnp.where(lane == home, low, jnp.where(lane == home + 1, high, 0.0))
     mine = jnp.sum(mine, axis=0, keepdims=True)
     fin_own[...] = mine
-    fin[d] = mine
-
-    def f_copy(q, r):
+    keep = pltpu.make_async_copy(fin_own, fin.at[d], out_sem.at[0])
+    keep.start()
+
+    def f_copy(to_z, r):
         return pltpu.make_async_remote_copy(
             src_ref=fin_own, dst_ref=fin.at[d], send_sem=f_send, recv_sem=f_recv,
-            device_id=(lax.rem(z + q, NZ) * NX + lax.rem(xd + r, NX), y), device_id_type=MESH)
-
-    pairs = [(q, r) for q in FAR for r in FAR if q or r]
-    for q, r in pairs:
-        f_copy(q, r).start()
+            device_id=(to_z * NX + lax.rem(xd + r, NX), y), device_id_type=MESH)
+
+    for to_z in range(NZ):
+        for r in FAR[:-1]:
+            f_copy(to_z, r).start()
+
+        @pl.when(z != to_z)
+        def _():
+            f_copy(to_z, 0).start()
 
     s = lf[2]
     for r in range(NZ - 1):
         s = s + lfz[r]
-    for n in range(NODES):
-        tot = s[:, 64:128]
-        lft = s[:, 0:64]
-        for side, part in enumerate((lft, tot - lft)):
-            g = part[:, n * K:(n + 1) * K]
-            h = part[:, 32 + n:33 + n]
-            leaf_ref[2 * n + side:2 * n + side + 1, :] = -g / (h + LAMBDA_REG)
+    leaf_v[...] = s
+    keep_leaf = pltpu.make_async_copy(leaf_v, leaf_sum, out_sem.at[1])
+    keep_leaf.start()
 
     for c in first + second:
         c.wait_send()
@@ -340,7 +370,13 @@
 
     others = fin.at[pl.ds(0, NX * NZ - 1)]
     pltpu.make_async_copy(others, others, f_recv).wait()
-    lane1 = iota((1, 128), 1)
+    pltpu.make_async_copy(others, others, f_send).wait()
+    keep.wait()
+    keep_leaf.wait()
+
+
+def assemble(fin, leaf_sum, best_ref, leaf_ref):
+    lane = iota((1, 128), 1)
     for j in range(COLS):
         pair = []
         for q in (2 * j, 2 * j + 1):
@@ -348,10 +384,17 @@
             for r in range(1, NX):
                 v = v + fin[q * NX + r]
             pair.append(v)
-        best_ref[0:1, j * 128:(j + 1) * 128] = jnp.where(lane1 < 64, pair[0], pair[1])
+        best_ref[0:1, j * 128:(j + 1) * 128] = jnp.where(lane < 64, pair[0], pair[1])
         best_ref[1:2, j * 128:(j + 1) * 128] = pltpu.roll(
-            jnp.where(lane1 < 64, pair[1], pair[0]), 64, axis=1)
-    pltpu.make_async_copy(others, others, f_send).wait()
+            jnp.where(lane < 64, pair[1], pair[0]), 64, axis=1)
+    s = leaf_sum[...]
+    tot = s[:, 64:128]
+    lft = s[:, 0:64]
+    for n in range(NODES):
+        for side, part in enumerate((lft, tot - lft)):
+            g = part[:, n * K:(n + 1) * K]
+            h = part[:, 32 + n:33 + n]
+            leaf_ref[2 * n + side:2 * n + side + 1, :] = -g / (h + LAMBDA_REG)
 
 
 def shards(table, sample_rows, gradients, hessian, node_ids, split_feature, split_bin):
@@ -359,14 +402,14 @@
     hbm = pl.BlockSpec(memory_space=pltpu.HBM)
     dma = pltpu.SemaphoreType.DMA
     row = pltpu.VMEM((1, 128), F32)
-    return pl.pallas_call(
+    fin, leaf_sum = pl.pallas_call(
         kernel,
         out_shape=(
-            jax.ShapeDtypeStruct((NODES, WIDTH), F32),
-            jax.ShapeDtypeStruct((2 * NODES, K), F32),
+            jax.ShapeDtypeStruct((NX * NZ, 1, 128), F32),
+            jax.ShapeDtypeStruct((1, 128), F32),
         ),
         in_specs=[hbm] * 7,
-        out_specs=(vmem, vmem),
+        out_specs=(hbm, hbm),
         scratch_shapes=[
             pltpu.SMEM((NODES,), jnp.int32),
             pltpu.SMEM((NODES,), jnp.int32),
@@ -386,7 +429,7 @@
             pltpu.VMEM((NY - 1, 1, 128), F32),
             pltpu.VMEM((NX - 1, 1, 128), F32),
             pltpu.VMEM((NZ - 1, 1, 128), F32),
-            pltpu.VMEM((NX * NZ, 1, 128), F32),
+            row,
             row,
             dma((6,)), dma((COLS,)),
             dma((NZ,)), dma((NZ,)),
@@ -395,6 +438,8 @@
             dma((NZ - 1,)), dma((NZ - 1,)),
             dma((3,)), dma((3,)),
             dma, dma,
+            dma((2,)),
+            pltpu.SemaphoreType.REGULAR((3,)),
         ],
         compiler_params=pltpu.CompilerParams(
             collective_id=0, has_side_effects=True, vmem_limit_bytes=60 * 2**20),
@@ -402,6 +447,16 @@
         split_feature, split_bin, table, sample_rows.reshape(1, S), gradients.T,
         hessian.reshape(COLS, 128), node_ids.reshape(1, S),
     )
+    return pl.pallas_call(
+        assemble,
+        out_shape=(
+            jax.ShapeDtypeStruct((NODES, WIDTH), F32),
+            jax.ShapeDtypeStruct((2 * NODES, K), F32),
+        ),
+        in_specs=[vmem, vmem],
+        out_specs=(vmem, vmem),
+        compiler_params=pltpu.CompilerParams(vmem_limit_bytes=60 * 2**20),
+    )(fin, leaf_sum)
 
 
 def solution(mesh):

time: 40.9 us -> 40.2 us (0.983)
  local copies, waits for them, and re-layouts: 2.5 us -> 0 us
  Pallas kernels: 37.6 us -> 39.3 us
    unnamed x2 -> x0, local copies, waits for them, and re-layouts: 2.5 us -> none
    pallas_call x1 -> x2, Pallas kernels: 37.6 us -> 39.3 us  [the longest x1 37.8 us: shards(): pl.pallas_call(kernel, out_shape=(jax.ShapeDtypeStruct((NX * NZ, 1, 128),...]
where the time goes in v3:
time: 40.2 us; the launch traced here: 40 us
  Pallas kernels  39.3 us (98%)
  between operations  0.64 us (2%)
    pallas_call x1, Pallas kernels, shards(): pl.pallas_call(kernel, out_shape=(jax.ShapeDtypeStruct((NX * NZ, 1, 128),...  37.8 us
    pallas_call x1, Pallas kernels, shards(): pl.pallas_call(assemble, out_shape=(jax.ShapeDtypeStruct((NODES, WIDTH),...  1.56 us

profile of v3, /device:TPU:1, one launch (start us, length us, event | category | flops | bytes accessed | tf_op | source)
XLA Modules:
  0.0 40.0 jit_solution(7929934117994477220)
XLA Ops:
  0.6 37.8 %shard_map.86 = (f32[64,1,128]{2,1,0:T(1,128)}, f32[1,128]{1,0:T(1,128)}) custom-call(s32[2]{0:T(128)} %sf_hbm.1, s32[2]{0:T(128)} %sb_hbm.1, s32[1024,512]{1,0:T(8,128)} %table_hbm.1, s32[1,512]{1,0:T(1,128)} %bitcast.5, bf16[16,512]{1,0:T(8,128)(2,1)} %bitcast.4, bf16[4,128]{1,0:T(4,128)(2,1)} %bitcast.7, s32[1,512]{1,0:T(1,128)} %bitcast.6), custom_call_target="tpu_custom_call" | custom-call | tf_op jit(solution)/shard_map/pallas_call | solution.py:405
  38.4 1.6 %shard_map.87 = (f32[2,512]{1,0:T(2,128)}, f32[4,16]{1,0:T(4,128)}) custom-call(f32[64,1,128]{2,1,0:T(1,128)} %get-tuple-element.4.fin, f32[1,128]{1,0:T(1,128)} %get-tuple-element.5.leaf_sum), custom_call_target="tpu_custom_call" | custom-call | tf_op jit(solution)/shard_map/pallas_call | solution.py:450

commit v4 on v3

--- a/solution.py
+++ b/solution.py
@@ -21,7 +21,7 @@
 COLS = WIDTH // 128
 WROWS = 48
 HROWS = COLS * 32 + 8
-AHEAD = 3
+AHEAD = 4
 FAR = (4, 3, 5, 2, 6, 1, 7, 0)
 MESH = pl.DeviceIdType.MESH
 F32 = jnp.float32
@@ -160,7 +160,7 @@
             for c in first:
                 c.start()
         for i in (2 * j, 2 * j + 1):
-            if i < AHEAD:
+            if i < 2:
                 start_chunk(i)
             x_copy(i, 0, True).start()
         if j == 0:
@@ -226,11 +226,12 @@
     for r in range(1, NY):
         l_copy(0, lfy.at[NY - r - 1], ypeer(r)).start()
 
-    for c in first[:3]:
-        c.wait_recv()
     second = [ch_copy(m, 4 + m, sibling, 3 + m) for m in range(1, 4)]
-    for c in second:
-        c.start()
+    for m in (3, 1, 2):
+        first[3 - m].wait_recv()
+        second[m - 1].start()
+    for i in range(2,4):
+        start_chunk(i)
 
     first[3].wait_recv()
     weights(4, 4)

time: 40.2 us -> 39.4 us (0.980)
  Pallas kernels: 39.3 us -> 38.6 us
    pallas_call x1, Pallas kernels: 37.8 us -> 37 us  [shards(): pl.pallas_call(kernel, out_shape=(jax.ShapeDtypeStruct((NX * NZ, 1, 128),...]
where the time goes in v4:
time: 39.4 us; the launch traced here: 39.2 us
  Pallas kernels  38.6 us (98%)
  between operations  0.64 us (2%)
    pallas_call x1, Pallas kernels, shards(): pl.pallas_call(kernel, out_shape=(jax.ShapeDtypeStruct((NX * NZ, 1, 128),...  37 us
    pallas_call x1, Pallas kernels, shards(): pl.pallas_call(assemble, out_shape=(jax.ShapeDtypeStruct((NODES, WIDTH),...  1.56 us

profile of v4, /device:TPU:1, one launch (start us, length us, event | category | flops | bytes accessed | tf_op | source)
XLA Modules:
  0.0 39.2 jit_solution(4667351756103402058)
XLA Ops:
  0.6 37.0 %shard_map.86 = (f32[64,1,128]{2,1,0:T(1,128)}, f32[1,128]{1,0:T(1,128)}) custom-call(s32[2]{0:T(128)} %sf_hbm.1, s32[2]{0:T(128)} %sb_hbm.1, s32[1024,512]{1,0:T(8,128)} %table_hbm.1, s32[1,512]{1,0:T(1,128)} %bitcast.5, bf16[16,512]{1,0:T(8,128)(2,1)} %bitcast.4, bf16[4,128]{1,0:T(4,128)(2,1)} %bitcast.7, s32[1,512]{1,0:T(1,128)} %bitcast.6), custom_call_target="tpu_custom_call" | custom-call | tf_op jit(solution)/shard_map/pallas_call | solution.py:406
  37.7 1.6 %shard_map.87 = (f32[2,512]{1,0:T(2,128)}, f32[4,16]{1,0:T(4,128)}) custom-call(f32[64,1,128]{2,1,0:T(1,128)} %get-tuple-element.4.fin, f32[1,128]{1,0:T(1,128)} %get-tuple-element.5.leaf_sum), custom_call_target="tpu_custom_call" | custom-call | tf_op jit(solution)/shard_map/pallas_call | solution.py:451

commit v5 on v4

--- a/solution.py
+++ b/solution.py
@@ -47,7 +47,7 @@
     sf_hbm, sb_hbm, table_hbm, rows_hbm, grad_hbm, hess_hbm, node_hbm,
     fin, leaf_sum,
     sf, sb, tab, rows_v, grad_v, hess_v, node_v, pk, rx, blob, wt, acc, zs, rz,
-    lf, lfy, lfx, lfz, fin_own, leaf_v,
+    lf, lfy, lfx, lfz, lff, fin_own, leaf_v,
     in_sem, tab_sem, rx_send, rx_recv, sib_send, sib_recv, ch_send, ch_recv, rz_send, rz_recv,
     l_send, l_recv, f_send, f_recv, out_sem, hello,
 ):
@@ -97,8 +97,11 @@
         pl.semaphore_signal(barrier, inc=1, device_id=zpeer(r), device_id_type=MESH)
     for r in range(1, NX):
         pl.semaphore_signal(barrier, inc=1, device_id=xpeer(r), device_id_type=MESH)
-    for r in range(1, NY):
-        pl.semaphore_signal(barrier, inc=1, device_id=ypeer(r), device_id_type=MESH)
+
+    @pl.when(z == 0)
+    def _():
+        for r in range(1, NY):
+            pl.semaphore_signal(barrier, inc=1, device_id=ypeer(r), device_id_type=MESH)
 
     def greet(k):
         for r in (1, NZ - 1):
@@ -156,7 +159,7 @@
         pk[pl.ds(col(j), 128), :] = lax.dot_general(
             part, hot, (((0,), (0,)), ((), ())), preferred_element_type=F32)
         if j == 0:
-            pl.semaphore_wait(barrier, NX + NY)
+            pl.semaphore_wait(barrier, jnp.where(z == 0, NX + NY, NX + 1))
             for c in first:
                 c.start()
         for i in (2 * j, 2 * j + 1):
@@ -223,8 +226,8 @@
             src_ref=lf.at[stage], dst_ref=dst, send_sem=l_send.at[stage], recv_sem=l_recv.at[stage],
             device_id=where, device_id_type=MESH)
 
-    for r in range(1, NY):
-        l_copy(0, lfy.at[NY - r - 1], ypeer(r)).start()
+    for r in range(1, NX):
+        l_copy(0, lfx.at[NX - r - 1], xpeer(r)).start()
 
     second = [ch_copy(m, 4 + m, sibling, 3 + m) for m in range(1, 4)]
     for m in (3, 1, 2):
@@ -288,25 +291,29 @@
 
         @pl.when(i == 1)
         def _():
-            pltpu.make_async_copy(lfy, lfy, l_recv.at[0]).wait()
-            lf[1] = lf[0] + lfy[0] + lfy[1] + lfy[2]
-            for r in range(1, NX):
-                l_copy(1, lfx.at[NX - r - 1], xpeer(r)).start()
-
-        @pl.when(i == 4)
-        def _():
-            pltpu.make_async_copy(lfx, lfx, l_recv.at[1]).wait()
-            s = lf[1]
+            pltpu.make_async_copy(lfx, lfx, l_recv.at[0]).wait()
+            s = lf[0]
             for r in range(NX - 1):
                 s = s + lfx[r]
+            lf[1] = s
+
+        @pl.when((i == 1) & (z != 0))
+        def _():
+            l_copy(1, lfz.at[z - 1], (xd, y)).start()
+
+        @pl.when((i == 6) & (z == 0))
+        def _():
+            pltpu.make_async_copy(lfz, lfz, l_recv.at[1]).wait()
+            s = lf[1]
+            for r in range(NZ - 1):
+                s = s + lfz[r]
             lf[2] = s
-            for r in range(1, NZ):
-                l_copy(2, lfz.at[NZ - r - 1], zpeer(r)).start()
+            for r in range(1, NY):
+                l_copy(2, lfy.at[NY - r - 1], ypeer(r)).start()
 
         return carry
 
     lax.fori_loop(0, NZ, chunk, 0)
-    pltpu.make_async_copy(lfz, lfz, l_recv.at[2]).wait()
     for i in (3, 4, 5, 6):
         pltpu.make_async_copy(rz.at[i], rz.at[i], rz_recv.at[i]).wait()
     left = zs[7] + rz[3] + rz[4] + rz[5] + rz[6]
@@ -350,10 +357,20 @@
         def _():
             f_copy(to_z, 0).start()
 
-    s = lf[2]
-    for r in range(NZ - 1):
-        s = s + lfz[r]
-    leaf_v[...] = s
+    @pl.when(z == 0)
+    def _():
+        pltpu.make_async_copy(lfy, lfy, l_recv.at[2]).wait()
+        s = lf[2] + lfy[0] + lfy[1] + lfy[2]
+        lf[3] = s
+        for r in FAR[:-1]:
+            l_copy(3, lff, zpeer(r)).start()
+        leaf_v[...] = s
+
+    @pl.when(z != 0)
+    def _():
+        pltpu.make_async_copy(lff, lff, l_recv.at[3]).wait()
+        leaf_v[...] = lff[...]
+
     keep_leaf = pltpu.make_async_copy(leaf_v, leaf_sum, out_sem.at[1])
     keep_leaf.start()
 
@@ -365,9 +382,16 @@
     pltpu.make_async_copy(rx.at[0], rx.at[0], sib_send).wait()
     for i in range(NZ - 1):
         pltpu.make_async_copy(rz.at[i], rz.at[i], rz_send.at[i]).wait()
-    pltpu.make_async_copy(lfy, lfy, l_send.at[0]).wait()
-    pltpu.make_async_copy(lfx, lfx, l_send.at[1]).wait()
-    pltpu.make_async_copy(lfz, lfz, l_send.at[2]).wait()
+    pltpu.make_async_copy(lfx, lfx, l_send.at[0]).wait()
+
+    @pl.when(z != 0)
+    def _():
+        pltpu.make_async_copy(lff, lff, l_send.at[1]).wait()
+
+    @pl.when(z == 0)
+    def _():
+        pltpu.make_async_copy(lfy, lfy, l_send.at[2]).wait()
+        pltpu.make_async_copy(lfz, lfz, l_send.at[3]).wait()
 
     others = fin.at[pl.ds(0, NX * NZ - 1)]
     pltpu.make_async_copy(others, others, f_recv).wait()
@@ -426,10 +450,11 @@
             pltpu.VMEM((NZ, WROWS, OWN * BINS), F32),
             pltpu.VMEM((NZ, HROWS, 128), F32),
             pltpu.VMEM((NZ - 1, HROWS, 128), F32),
-            pltpu.VMEM((3, 1, 128), F32),
+            pltpu.VMEM((4, 1, 128), F32),
             pltpu.VMEM((NY - 1, 1, 128), F32),
             pltpu.VMEM((NX - 1, 1, 128), F32),
             pltpu.VMEM((NZ - 1, 1, 128), F32),
+            row,
             row,
             row,
             dma((6,)), dma((COLS,)),
@@ -437,7 +462,7 @@
             dma, dma,
             dma((7,)), dma((8,)),
             dma((NZ - 1,)), dma((NZ - 1,)),
-            dma((3,)), dma((3,)),
+            dma((4,)), dma((4,)),
             dma, dma,
             dma((2,)),
             pltpu.SemaphoreType.REGULAR((3,)),

time: 39.4 us -> 38.1 us (0.967)
  Pallas kernels: 38.6 us -> 37.3 us
    pallas_call x1, Pallas kernels: 37 us -> 35.7 us  [shards(): pl.pallas_call(kernel, out_shape=(jax.ShapeDtypeStruct((NX * NZ, 1, 128),...]
where the time goes in v5:
time: 38.1 us; the launch traced here: 37.9 us
  Pallas kernels  37.3 us (98%)
  between operations  0.64 us (2%)
    pallas_call x1, Pallas kernels, shards(): pl.pallas_call(kernel, out_shape=(jax.ShapeDtypeStruct((NX * NZ, 1, 128),...  35.7 us
    pallas_call x1, Pallas kernels, shards(): pl.pallas_call(assemble, out_shape=(jax.ShapeDtypeStruct((NODES, WIDTH),...  1.56 us

profile of v5, /device:TPU:1, one launch (start us, length us, event | category | flops | bytes accessed | tf_op | source)
XLA Modules:
  0.0 37.9 jit_solution(153626513045441521)
XLA Ops:
  0.6 35.7 %shard_map.86 = (f32[64,1,128]{2,1,0:T(1,128)}, f32[1,128]{1,0:T(1,128)}) custom-call(s32[2]{0:T(128)} %sf_hbm.1, s32[2]{0:T(128)} %sb_hbm.1, s32[1024,512]{1,0:T(8,128)} %table_hbm.1, s32[1,512]{1,0:T(1,128)} %bitcast.5, bf16[16,512]{1,0:T(8,128)(2,1)} %bitcast.4, bf16[4,128]{1,0:T(4,128)(2,1)} %bitcast.7, s32[1,512]{1,0:T(1,128)} %bitcast.6), custom_call_target="tpu_custom_call" | custom-call | tf_op jit(solution)/shard_map/pallas_call | solution.py:430
  36.3 1.6 %shard_map.87 = (f32[2,512]{1,0:T(2,128)}, f32[4,16]{1,0:T(4,128)}) custom-call(f32[64,1,128]{2,1,0:T(1,128)} %get-tuple-element.4.fin, f32[1,128]{1,0:T(1,128)} %get-tuple-element.5.leaf_sum), custom_call_target="tpu_custom_call" | custom-call | tf_op jit(solution)/shard_map/pallas_call | solution.py:476

commit v6 on v5

--- a/solution.py
+++ b/solution.py
@@ -289,7 +289,7 @@
             zs[c] = zs[c] + rz[c - 2]
             z_copy(c).start()
 
-        @pl.when(i == 1)
+        @pl.when(i == 2)
         def _():
             pltpu.make_async_copy(lfx, lfx, l_recv.at[0]).wait()
             s = lf[0]
@@ -297,7 +297,7 @@
                 s = s + lfx[r]
             lf[1] = s
 
-        @pl.when((i == 1) & (z != 0))
+        @pl.when((i == 2) & (z != 0))
         def _():
             l_copy(1, lfz.at[z - 1], (xd, y)).start()
 

time: 38.1 us -> 38.1 us (level)
  no operation moved by 1% of the time
where the time goes in v6:
time: 38.1 us; the launch traced here: 37.9 us
  Pallas kernels  37.3 us (98%)
  between operations  0.64 us (2%)
    pallas_call x1, Pallas kernels, shards(): pl.pallas_call(kernel, out_shape=(jax.ShapeDtypeStruct((NX * NZ, 1, 128),...  35.7 us
    pallas_call x1, Pallas kernels, shards(): pl.pallas_call(assemble, out_shape=(jax.ShapeDtypeStruct((NODES, WIDTH),...  1.56 us

profile of v6, /device:TPU:1, one launch (start us, length us, event | category | flops | bytes accessed | tf_op | source)
XLA Modules:
  0.0 37.9 jit_solution(256161316432301629)
XLA Ops:
  0.6 35.7 %shard_map.86 = (f32[64,1,128]{2,1,0:T(1,128)}, f32[1,128]{1,0:T(1,128)}) custom-call(s32[2]{0:T(128)} %sf_hbm.1, s32[2]{0:T(128)} %sb_hbm.1, s32[1024,512]{1,0:T(8,128)} %table_hbm.1, s32[1,512]{1,0:T(1,128)} %bitcast.5, bf16[16,512]{1,0:T(8,128)(2,1)} %bitcast.4, bf16[4,128]{1,0:T(4,128)(2,1)} %bitcast.7, s32[1,512]{1,0:T(1,128)} %bitcast.6), custom_call_target="tpu_custom_call" | custom-call | tf_op jit(solution)/shard_map/pallas_call | solution.py:430
  36.3 1.6 %shard_map.87 = (f32[2,512]{1,0:T(2,128)}, f32[4,16]{1,0:T(4,128)}) custom-call(f32[64,1,128]{2,1,0:T(1,128)} %get-tuple-element.4.fin, f32[1,128]{1,0:T(1,128)} %get-tuple-element.5.leaf_sum), custom_call_target="tpu_custom_call" | custom-call | tf_op jit(solution)/shard_map/pallas_call | solution.py:476
